TPU v7x, 32 devices: a whole 2x2x4 slice. The times are simulated.
32 devices in a mesh: grp: 2 (over x), ev: 4 (over y, core), hd: 4 (over z).
Axes of the slice: x: 2, y: 2, z: 4, core: 2. Of those that a mesh axis runs over, the one named last changes fastest.
Arguments:
- hist_keys: bfloat16 [8, 16384, 1024], P('grp', 'ev', 'hd'), parts along dimension 0, may hold values from -6 to 6
- hist_values: bfloat16 [8, 16384, 1024], P('grp', 'ev', 'hd'), parts along dimension 0, may hold values from -6 to 6
- hist_len: int32 [8], P('grp'), parts along dimension 0, may hold values from 4096 to 16384
- new_queries: bfloat16 [8, 1024, 1024], P('grp', 'ev', 'hd'), parts along dimension 0, may hold values from -6 to 6
- event_gate: bfloat16 [8, 1024, 1024], P('grp', 'ev', 'hd'), parts along dimension 0, may hold values from -6 to 6
- key_weight: bfloat16 [1024, 1024], P(None, 'hd'), may hold values from -0.1875 to 0.1875
- value_weight: bfloat16 [1024, 1024], P(None, 'hd'), may hold values from -0.1875 to 0.1875
- event_gain: float32 [1024], P('hd'), may hold values from 0.25 to 1.75
- cand_queries: bfloat16 [4096, 1024], P(('grp', 'ev'), 'hd'), parts along dimension 0, may hold values from -6 to 6
- cand_gate: bfloat16 [4096, 1024], P(('grp', 'ev'), 'hd'), parts along dimension 0, may hold values from -6 to 6
- cand_gain: float32 [1024], P('hd'), may hold values from 0.25 to 1.75
- block_user: int32 [32], P(('grp', 'ev')), parts along dimension 0, may hold values from 0 to 3, as said below
- cand_count: int32 [8], P('grp'), parts along dimension 0, may hold values from 1 to 1024, as said below
Outputs:
- event_out: bfloat16 [8, 1024, 1024], P('grp', 'ev', 'hd'), parts along dimension 0
- cand_out: bfloat16 [4096, 1024], P(('grp', 'ev'), 'hd'), parts along dimension 0
There are 2 independent parts, one for each index of `grp`. A program takes and returns all parts, laid end to end along the dimension named above; an argument that names none is the same for every part. Nothing has to cross between parts.
Inputs may be any that keep to these rules, and one draw needn't show every extreme that they name: `block_user`: blocks belong to users in order: the first ceil(cand_count[0] / 128) blocks to user 0, the next ceil(cand_count[1] / 128) to user 1, and so on; every user has at least one block and all 16 blocks are used. `cand_count`: the blocks of users add up to 16 as stated for block_user; one user has exactly 8 full blocks.
All inputs are finite; a program needn't handle non-finite values.
Results may differ from a plain program's by a relative error of at most 0.0072.
Values may be sent and summed in bfloat16 or wider, within the bound.
A program may use at most 128 MiB of HBM per device.

v0:
```python
import jax
import jax.numpy as jnp
from jax import lax
from jax.sharding import PartitionSpec as P

HEAD = 128
BLOCK = 128


EPSILON = 1e-05


def head_norm(values, gain):
    centre = jnp.mean(values, axis=-1, keepdims=True)
    shifted = values - centre
    spread = jnp.mean(shifted * shifted, axis=-1, keepdims=True)
    return shifted * lax.rsqrt(spread + EPSILON) * gain


def local(
    hist_keys,
    hist_values,
    hist_len,
    new_queries,
    event_gate,
    key_weight,
    value_weight,
    event_gain,
    cand_queries,
    cand_gate,
    cand_gain,
    block_user,
    cand_count,
):
    n_users, hist_rows, col_width = hist_keys.shape
    n_heads = col_width // HEAD
    score_scale = HEAD ** (-0.5)
    key_block = min(1024, hist_rows)
    n_blocks = hist_rows // key_block
    keys_split = hist_keys.reshape(n_users, n_blocks, key_block, n_heads, HEAD)
    values_split = hist_values.reshape(n_users, n_blocks, key_block, n_heads, HEAD)
    event_base = lax.axis_index("ev") * hist_rows
    pieces = lax.all_gather(new_queries, "ev", axis=1, tiled=True)
    n_rows = pieces.shape[1]
    queries_here = pieces.reshape(n_users, n_rows, n_heads, HEAD)

    def history_step(total, block_idx):
        keys_here = lax.dynamic_index_in_dim(keys_split, block_idx, 1, keepdims=False)
        values_here = lax.dynamic_index_in_dim(values_split, block_idx, 1, keepdims=False)
        scores = (
            jnp.einsum(
                "unhd,ukhd->uhnk", queries_here, keys_here, preferred_element_type=jnp.float32
            )
            * score_scale
        )
        position = event_base + block_idx * key_block + jnp.arange(key_block, dtype=jnp.int32)
        alive = (position[None, :] < hist_len[:, None]).astype(jnp.float32)
        weights = (jax.nn.silu(scores) * alive[:, None, None, :]).astype(jnp.bfloat16)
        return (
            total
            + jnp.einsum(
                "uhnk,ukhd->unhd", weights, values_here, preferred_element_type=jnp.float32
            ),
            None,
        )

    total, _ = lax.scan(
        history_step,
        jnp.zeros((n_users, n_rows, n_heads, HEAD), jnp.float32),
        jnp.arange(n_blocks, dtype=jnp.int32),
    )
    partial_sum = total.reshape(n_users, n_rows, col_width)
    blocks_here = block_user.shape[0]
    cand_split = cand_queries.reshape(blocks_here, BLOCK, n_heads, HEAD)
    user_ids = jnp.arange(n_users, dtype=jnp.int32)
    owner_table = block_user[:, None] == user_ids[None, :]
    owner_pick = owner_table.astype(jnp.bfloat16)
    attended = lax.psum_scatter(partial_sum, "ev", scatter_dimension=1, tiled=True)
    rows_here = attended.shape[1]
    shaped = attended.reshape(n_users, rows_here, n_heads, HEAD)
    gate_f = event_gate.astype(jnp.float32).reshape(n_users, rows_here, n_heads, HEAD)
    event_out = (
        (head_norm(shaped, event_gain.reshape(n_heads, HEAD)) * gate_f)
        .astype(jnp.bfloat16)
        .reshape(n_users, rows_here, col_width)
    )
    rows_here = event_out.shape[1]
    flat = event_out.reshape(n_users * rows_here, col_width)
    pieces = lax.all_gather(flat, "hd", axis=1, tiled=True)
    key_sum = jnp.dot(pieces, key_weight, preferred_element_type=jnp.float32)
    value_sum = jnp.dot(pieces, value_weight, preferred_element_type=jnp.float32)
    fresh_keys = key_sum.astype(jnp.bfloat16).reshape(n_users, rows_here, col_width)
    fresh_values = value_sum.astype(jnp.bfloat16).reshape(n_users, rows_here, col_width)
    keys_piece = lax.all_gather(fresh_keys, "ev", axis=1, tiled=True)
    values_piece = lax.all_gather(fresh_values, "ev", axis=1, tiled=True)
    n_rows = keys_piece.shape[1]
    keys_own = jnp.dot(
        owner_pick,
        keys_piece.reshape(n_users, n_rows * col_width),
        preferred_element_type=jnp.float32,
    )
    keys_own = keys_own.astype(jnp.bfloat16).reshape(blocks_here, n_rows, n_heads, HEAD)
    values_own = jnp.dot(
        owner_pick,
        values_piece.reshape(n_users, n_rows * col_width),
        preferred_element_type=jnp.float32,
    )
    values_own = values_own.astype(jnp.bfloat16).reshape(blocks_here, n_rows, n_heads, HEAD)
    scores = (
        jnp.einsum("bchd,brhd->bhcr", cand_split, keys_own, preferred_element_type=jnp.float32)
        * score_scale
    )
    weights = jax.nn.silu(scores).astype(jnp.bfloat16)
    cand_attn = jnp.einsum(
        "bhcr,brhd->bchd", weights, values_own, preferred_element_type=jnp.float32
    )
    block_count = (cand_count + BLOCK - 1) // BLOCK
    first_block = jnp.cumsum(block_count) - block_count
    owner_int = owner_table.astype(jnp.int32)
    own_first = jnp.sum(owner_int * first_block[None, :], axis=1)
    own_limit = jnp.sum(owner_int * cand_count[None, :], axis=1)
    block_global = lax.axis_index("ev") * blocks_here + jnp.arange(blocks_here, dtype=jnp.int32)
    row_pos = (block_global - own_first)[:, None] * BLOCK + jnp.arange(BLOCK, dtype=jnp.int32)[
        None, :
    ]
    valid = (row_pos < own_limit[:, None]).astype(jnp.float32)
    gate_c = cand_gate.astype(jnp.float32).reshape(blocks_here, BLOCK, n_heads, HEAD)
    cand_out = (
        head_norm(cand_attn, cand_gain.reshape(n_heads, HEAD)) * gate_c * valid[:, :, None, None]
    ).astype(jnp.bfloat16)
    return (event_out, cand_out.reshape(blocks_here * BLOCK, col_width))


def solution(mesh):
    return jax.shard_map(
        local,
        mesh=mesh,
        in_specs=(
            P("grp", "ev", "hd"),
            P("grp", "ev", "hd"),
            P("grp"),
            P("grp", "ev", "hd"),
            P("grp", "ev", "hd"),
            P(None, "hd"),
            P(None, "hd"),
            P("hd"),
            P(("grp", "ev"), "hd"),
            P(("grp", "ev"), "hd"),
            P("hd"),
            P(("grp", "ev")),
            P("grp"),
        ),
        out_specs=(P("grp", "ev", "hd"), P(("grp", "ev"), "hd")),
        check_vma=False,
    )
```

profile of v0, /device:TPU:0, one launch (start us, length us, event | category | flops | bytes accessed | tf_op | source)
XLA Modules:
  0.0 361.2 jit_solution(16850112253524450805)
XLA Ops:
  7.2 2.1 copy.34
  9.4 12.7 %reshape.194 = bf16[4,4,1024,2,128]{4,3,2,1,0:T(2,128)(2,1)} reshape(bf16[4,4096,256]{2,1,0:T(8,128)(2,1)} %param.16) | data formatting | bytes 16777216 | tf_op jit(solution)/shard_map/reshape | solution.py:41
  22.1 12.5 %reshape.195 = bf16[4,4,1024,2,128]{4,3,2,1,0:T(2,128)(2,1)} reshape(bf16[4,4096,256]{2,1,0:T(8,128)(2,1)} %param.15) | data formatting | bytes 16777216 | tf_op jit(solution)/shard_map/reshape | solution.py:40
  35.7 4.0 %copy.37 = bf16[4,1024,2,128]{3,1,2,0:T(8,128)(2,1)} copy(bf16[4,1024,2,128]{1,3,2,0:T(8,128)(2,1)} %bitcast.111) | data formatting | bytes 4194304
  39.7 132.6 %while.11 = (s32[]{:T(128)}, f32[4,1024,2,128]{1,3,2,0:T(8,128)}, s32[4]{0:T(128)S(1)}, bf16[4,4,1024,2,128]{4,3,2,1,0:T(2,128)(2,1)}, bf16[4,4,1024,2,128]{4,3,...) while((s32[]{:T(128)}, f32[4,1024,2,128]{1,3,2,0:T(8,128)}, ...), condition=%wide.region_1.2_spmd.clone, body=%wide.region_0.1_spmd.clone.sunk | while | flops 4355793920 | bytes 27304156 | solution.py:67
  42.2 6.5 %constant_dynamic-slice_fusion.3 = (bf16[4,1,1024,2,128]{4,3,2,1,0:T(2,128)(2,1)}, bf16[4,1,1024,2,128]{4,3,2,1,0:T(2,128)(2,1)S(1)}) fusion(bf16[4,4,1024,2,128]{4,3,2,1,0:T(2,128)(2,1)} %get-tuple-element.191, s32[]{:T(128)S(6)} %select_n.18, bf16[4,4,1024,2,128]{4,3,2,1,0:T(2,128)(2,1)} %get-tuple-element.190), kind=kLoop, calls=%fused_computation.14.clone.1 | loop fusion | bytes 8388612 | tf_op jit(solution)/shard_map/while/body/eval_jaxpr/jit(dynamic_index_in_dim)/dynamic_slice | solution.py:48
  48.7 3.9 %copy.82 = bf16[4,1,1024,2,128]{2,4,3,0,1:T(8,128)(2,1)} copy(bf16[4,1,1024,2,128]{4,3,2,1,0:T(2,128)(2,1)S(1)} %get-tuple-element.162) | data formatting | bytes 4194304 | tf_op jit(solution)/shard_map/while/body/eval_jaxpr/jit(dynamic_index_in_dim)/dynamic_slice | solution.py:49
  53.3 19.0 %bitcast_add_fusion.2 = f32[4,1024,2,128]{1,3,2,0:T(8,128)} fusion(f32[4,1024,2,128]{1,3,2,0:T(8,128)} %get-tuple-element.176, f32[4,1024]{1,0:T(4,128)S(1)} %compare_convert_fusion.2, bf16[4,1024,2,128]{3,1,2,0:T(8,128)(2,1)} %get-tuple-element.192, bf16[4,1,1024,2,128]{4,3,2,1,0:T(2,128)(2,1)} %get-tuple-element.161, ...), kind=kOutput, calls=%fused_computation.8.clone.1 | convolution fusion | flops 4355784704 | bytes 14696449 | tf_op jit(solution)/shard_map/while/body/eval_jaxpr/uhnk,ukhd->unhd/dot_general | solution.py:61
  74.9 6.5 %constant_dynamic-slice_fusion.3 = (bf16[4,1,1024,2,128]{4,3,2,1,0:T(2,128)(2,1)}, bf16[4,1,1024,2,128]{4,3,2,1,0:T(2,128)(2,1)S(1)}) fusion(bf16[4,4,1024,2,128]{4,3,2,1,0:T(2,128)(2,1)} %get-tuple-element.191, s32[]{:T(128)S(6)} %select_n.18, bf16[4,4,1024,2,128]{4,3,2,1,0:T(2,128)(2,1)} %get-tuple-element.190), kind=kLoop, calls=%fused_computation.14.clone.1 | loop fusion | bytes 8388612 | tf_op jit(solution)/shard_map/while/body/eval_jaxpr/jit(dynamic_index_in_dim)/dynamic_slice | solution.py:48
  81.3 3.9 %copy.82 = bf16[4,1,1024,2,128]{2,4,3,0,1:T(8,128)(2,1)} copy(bf16[4,1,1024,2,128]{4,3,2,1,0:T(2,128)(2,1)S(1)} %get-tuple-element.162) | data formatting | bytes 4194304 | tf_op jit(solution)/shard_map/while/body/eval_jaxpr/jit(dynamic_index_in_dim)/dynamic_slice | solution.py:49
  86.0 19.7 %bitcast_add_fusion.2 = f32[4,1024,2,128]{1,3,2,0:T(8,128)} fusion(f32[4,1024,2,128]{1,3,2,0:T(8,128)} %get-tuple-element.176, f32[4,1024]{1,0:T(4,128)S(1)} %compare_convert_fusion.2, bf16[4,1024,2,128]{3,1,2,0:T(8,128)(2,1)} %get-tuple-element.192, bf16[4,1,1024,2,128]{4,3,2,1,0:T(2,128)(2,1)} %get-tuple-element.161, ...), kind=kOutput, calls=%fused_computation.8.clone.1 | convolution fusion | flops 4355784704 | bytes 14696449 | tf_op jit(solution)/shard_map/while/body/eval_jaxpr/uhnk,ukhd->unhd/dot_general | solution.py:61
  108.2 6.5 %constant_dynamic-slice_fusion.3 = (bf16[4,1,1024,2,128]{4,3,2,1,0:T(2,128)(2,1)}, bf16[4,1,1024,2,128]{4,3,2,1,0:T(2,128)(2,1)S(1)}) fusion(bf16[4,4,1024,2,128]{4,3,2,1,0:T(2,128)(2,1)} %get-tuple-element.191, s32[]{:T(128)S(6)} %select_n.18, bf16[4,4,1024,2,128]{4,3,2,1,0:T(2,128)(2,1)} %get-tuple-element.190), kind=kLoop, calls=%fused_computation.14.clone.1 | loop fusion | bytes 8388612 | tf_op jit(solution)/shard_map/while/body/eval_jaxpr/jit(dynamic_index_in_dim)/dynamic_slice | solution.py:48
  114.6 3.9 %copy.82 = bf16[4,1,1024,2,128]{2,4,3,0,1:T(8,128)(2,1)} copy(bf16[4,1,1024,2,128]{4,3,2,1,0:T(2,128)(2,1)S(1)} %get-tuple-element.162) | data formatting | bytes 4194304 | tf_op jit(solution)/shard_map/while/body/eval_jaxpr/jit(dynamic_index_in_dim)/dynamic_slice | solution.py:49
  119.3 19.7 %bitcast_add_fusion.2 = f32[4,1024,2,128]{1,3,2,0:T(8,128)} fusion(f32[4,1024,2,128]{1,3,2,0:T(8,128)} %get-tuple-element.176, f32[4,1024]{1,0:T(4,128)S(1)} %compare_convert_fusion.2, bf16[4,1024,2,128]{3,1,2,0:T(8,128)(2,1)} %get-tuple-element.192, bf16[4,1,1024,2,128]{4,3,2,1,0:T(2,128)(2,1)} %get-tuple-element.161, ...), kind=kOutput, calls=%fused_computation.8.clone.1 | convolution fusion | flops 4355784704 | bytes 14696449 | tf_op jit(solution)/shard_map/while/body/eval_jaxpr/uhnk,ukhd->unhd/dot_general | solution.py:61
  141.5 6.5 %constant_dynamic-slice_fusion.3 = (bf16[4,1,1024,2,128]{4,3,2,1,0:T(2,128)(2,1)}, bf16[4,1,1024,2,128]{4,3,2,1,0:T(2,128)(2,1)S(1)}) fusion(bf16[4,4,1024,2,128]{4,3,2,1,0:T(2,128)(2,1)} %get-tuple-element.191, s32[]{:T(128)S(6)} %select_n.18, bf16[4,4,1024,2,128]{4,3,2,1,0:T(2,128)(2,1)} %get-tuple-element.190), kind=kLoop, calls=%fused_computation.14.clone.1 | loop fusion | bytes 8388612 | tf_op jit(solution)/shard_map/while/body/eval_jaxpr/jit(dynamic_index_in_dim)/dynamic_slice | solution.py:48
  147.9 3.9 %copy.82 = bf16[4,1,1024,2,128]{2,4,3,0,1:T(8,128)(2,1)} copy(bf16[4,1,1024,2,128]{4,3,2,1,0:T(2,128)(2,1)S(1)} %get-tuple-element.162) | data formatting | bytes 4194304 | tf_op jit(solution)/shard_map/while/body/eval_jaxpr/jit(dynamic_index_in_dim)/dynamic_slice | solution.py:49
  152.6 19.7 %bitcast_add_fusion.2 = f32[4,1024,2,128]{1,3,2,0:T(8,128)} fusion(f32[4,1024,2,128]{1,3,2,0:T(8,128)} %get-tuple-element.176, f32[4,1024]{1,0:T(4,128)S(1)} %compare_convert_fusion.2, bf16[4,1024,2,128]{3,1,2,0:T(8,128)(2,1)} %get-tuple-element.192, bf16[4,1,1024,2,128]{4,3,2,1,0:T(2,128)(2,1)} %get-tuple-element.161, ...), kind=kOutput, calls=%fused_computation.8.clone.1 | convolution fusion | flops 4355784704 | bytes 14696449 | tf_op jit(solution)/shard_map/while/body/eval_jaxpr/uhnk,ukhd->unhd/dot_general | solution.py:61
  172.3 5.4 %copy.47 = f32[4,1024,256]{2,1,0:T(8,128)} copy(f32[4,1024,256]{1,2,0:T(8,128)} %bitcast.108) | data formatting | bytes 8388608 | tf_op jit(solution)/shard_map/reshape | solution.py:72
  177.7 46.3 %reduce-scatter.2.cloned.1.call-done = f32[4,256,256]{2,1,0:T(8,128)} async-done(((f32[4,1024,256]{2,1,0:T(8,128)}), f32[4,256,256]{2,1,0:T(8,128)}) %reduce-scatter.2.cloned.1.call-update) | async-done | bytes 1048592 | tf_op jit(solution)/shard_map/reduce_scatter | solution.py:78
  227.0 14.6 %multiply_reduce_fusion = f32[4,256,2]{2,1,0:T(8,128)S(1)} fusion(f32[4,256,2,128]{3,2,1,0:T(2,128)S(1)} %reshape.198, f32[4,256,2]{2,1,0:T(8,128)S(1)} %broadcast_multiply_fusion), kind=kLoop, calls=%fused_computation.38 | loop fusion | flops 784384 | bytes 1064960 | tf_op jit(solution)/shard_map/reduce_sum | solution.py:16
  246.2 46.3 %all-gather.7.cloned.1.call-done = bf16[1024,1024]{1,0:T(8,128)(2,1)} async-done(((bf16[1024,256]{1,0:T(8,128)(2,1)}), bf16[1024,1024]{1,0:T(8,128)(2,1)}) %all-gather.7.cloned.1.call-update) | async-done | bytes 2097168 | tf_op jit(solution)/shard_map/all_gather | solution.py:89
  292.6 3.1 convolution_convert_fusion.3
  295.8 3.3 convolution_convert_fusion.2
  306.3 3.1 sub.46
  309.4 2.3 multiply_convert_fusion
  311.7 5.0 %all-gather.9.cloned.1.call-done = bf16[4,1024,256]{2,1,0:T(8,128)(2,1)} async-done(((bf16[4,256,256]{2,1,0:T(8,128)(2,1)}), bf16[4,1024,256]{2,1,0:T(8,128)(2,1)}) %all-gather.9.cloned.1.call-update) | async-done | bytes 2097168 | tf_op jit(solution)/shard_map/all_gather | solution.py:95
  316.7 3.2 copy.52
  321.2 3.4 reshape.203
  324.7 16.2 %all-gather.11.cloned.1.call-done = bf16[4,1024,256]{2,1,0:T(8,128)(2,1)} async-done(((bf16[4,256,256]{2,1,0:T(8,128)(2,1)}), bf16[4,1024,256]{2,1,0:T(8,128)(2,1)}) %all-gather.11.cloned.1.call-update) | async-done | bytes 2097168 | tf_op jit(solution)/shard_map/all_gather | solution.py:94
  340.8 3.2 copy.53
  345.4 3.6 %reshape.206 = bf16[4,1024,2,128]{3,2,1,0:T(2,128)(2,1)} reshape(bf16[4,262144]{1,0:T(4,128)(2,1)S(1)} %convolution_convert_fusion) | data formatting | bytes 4194304 | tf_op jit(solution)/shard_map/reshape | solution.py:102
  349.0 4.5 %fusion.36 = (f32[4,128,2]{1,2,0:T(2,128)S(1)}, f32[4,128,2,128]{1,3,2,0:T(8,128)S(1)}) fusion(bf16[4,1024,2,128]{3,2,1,0:T(2,128)(2,1)} %reshape.206, bf16[4,128,2,128]{3,2,1,0:T(2,128)(2,1)S(1)} %copy-done.7, bf16[4,1024,2,128]{3,2,1,0:T(2,128)(2,1)} %reshape.203), kind=kOutput, calls=%fused_computation.62 | convolution fusion | flops 543292416 | bytes 4984832 | tf_op jit(solution)/shard_map/bhcr,brhd->bchd/dot_general | solution.py:114
  (76 shorter events, 22.4 us)
Async XLA Ops:
  7.2 285.4 %copy-start = (bf16[1024,256]{1,0:T(8,128)(2,1)S(1)}, bf16[1024,256]{1,0:T(8,128)(2,1)}, u32[]{:S(2)}) copy-start(bf16[1024,256]{1,0:T(8,128)(2,1)} %param.21) | copy-start | bytes 1572868
  7.2 28.5 %all-gather.5.cloned.1.call-start = ((), (), s32[]{:S(2)}) async-start(), calls=%async_computation.1 | async-start | bytes 2621440 | tf_op jit(solution)/shard_map/all_gather | solution.py:43
  9.3 214.7 %reduce-scatter.2.cloned.1.call-start = ((), (), s32[]{:S(2)}) async-start(), calls=%async_computation.2 | async-start | bytes 5242880 | tf_op jit(solution)/shard_map/reduce_scatter | solution.py:78
  35.7 4.0 %copy-start.8 = (s32[4]{0:T(128)S(1)}, s32[4]{0:T(128)}, u32[]{:S(2)}) copy-start(s32[4]{0:T(128)} %param.17) | copy-start | bytes 52
  177.7 114.9 %all-gather.7.cloned.1.call-start = ((), (), s32[]{:S(2)}) async-start(), calls=%async_computation.3 | async-start | bytes 2621440 | tf_op jit(solution)/shard_map/all_gather | solution.py:89
  241.5 3.6 copy-start.1
  241.5 3.6 copy-start.4
  241.5 3.6 copy-start.10
  244.1 1.0 copy-start.2
  246.2 70.5 %all-gather.9.cloned.1.call-start = ((), (), s32[]{:S(2)}) async-start(), calls=%async_computation.4 | async-start | bytes 2621440 | tf_op jit(solution)/shard_map/all_gather | solution.py:95
  295.7 5.1 %copy-start.12 = (s32[4]{0:T(128)S(1)}, s32[4]{0:T(128)}, u32[]{:S(2)}) copy-start(s32[4]{0:T(128)} %param.27) | copy-start | bytes 52
  295.7 5.3 %copy-start.6 = (bf16[512,256]{1,0:T(8,128)(2,1)S(1)}, bf16[512,256]{1,0:T(8,128)(2,1)}, u32[]{:S(2)}) copy-start(bf16[512,256]{1,0:T(8,128)(2,1)} %param.24) | copy-start | bytes 786436
  295.8 45.1 %all-gather.11.cloned.1.call-start = ((), (), s32[]{:S(2)}) async-start(), calls=%async_computation.5 | async-start | bytes 2621440 | tf_op jit(solution)/shard_map/all_gather | solution.py:94
  299.1 5.1 %copy-start.9 = (s32[4]{0:T(128)S(1)}, s32[4]{0:T(128)}, u32[]{:S(2)}) copy-start(s32[4]{0:T(128)} %param.26) | copy-start | bytes 52
  306.3 3.1 copy-start.3
  345.4 3.6 %copy-start.7 = (bf16[4,128,2,128]{3,2,1,0:T(2,128)(2,1)S(1)}, bf16[4,128,2,128]{3,2,1,0:T(2,128)(2,1)}, u32[]{:S(2)}) copy-start(bf16[4,128,2,128]{3,2,1,0:T(2,128)(2,1)} %reshape.207) | copy-start | bytes 786436
  349.0 4.6 %copy-start.5 = (f32[4,128,2,128]{1,3,2,0:T(8,128)S(1)}, f32[4,128,2,128]{1,3,2,0:T(8,128)}, u32[]{:S(2)}) copy-start(f32[4,128,2,128]{1,3,2,0:T(8,128)} %copy.43) | copy-start | bytes 1572868
  349.0 4.6 %copy-start.11 = (f32[256]{0:T(256)S(1)}, f32[256]{0:T(256)}, u32[]{:S(2)}) copy-start(f32[256]{0:T(256)} %param.25) | copy-start | bytes 3076
Sparse Core Ops, SparseCore 0:
  10.1 25.5 all-gather.4
  177.8 46.1 reduce-scatter.1
  246.3 46.2 all-gather.6
  295.9 20.8 all-gather.8
  318.2 22.5 all-gather.10
where the time goes:
time: 363 us; the launch traced here: 361 us
  waiting for transfers between devices  115 us (32%)
  local copies, waits for them, and re-layouts  110 us (30%)
  matrix products  91.5 us (25%)
  other arithmetic  20.2 us (6%)
  between operations  14 us (4%)
  loops' own time  10.4 us (3%)
    dot_general x4, matrix products, history_step(): jnp.einsum('uhnk,ukhd->unhd', weights, values_here, preferred_element_typ...  78.1 us
    all_gather x1, waiting for transfers between devices, local(): pieces = lax.all_gather(flat, 'hd', axis=1, tiled=True)  46.3 us
    reduce_scatter x1, waiting for transfers between devices, local(): lax.psum_scatter(partial_sum, 'ev', scatter_dimension=1, tiled=True)  46.3 us
    dynamic_slice x4, local copies, waits for them, and re-layouts, history_step(): lax.dynamic_index_in_dim(keys_split, block_idx, 1, keepdims=False)  25.9 us
    all_gather x1, waiting for transfers between devices, local(): keys_piece = lax.all_gather(fresh_keys, 'ev', axis=1, tiled=True)  16.2 us
    dynamic_slice x4, local copies, waits for them, and re-layouts, history_step(): lax.dynamic_index_in_dim(values_split, block_idx, 1, keepdims=False)  15.6 us
    reduce_sum x2, other arithmetic, head_norm(): spread = jnp.mean(shifted * shifted, axis=-1, keepdims=True)  14.6 us
    unnamed x31, local copies, waits for them, and re-layouts  14.3 us
  transfers between devices with their start and end apart: 5, of which 5 were waited for; matrix products, arithmetic and copies ran while one was open for 14% of the time, Pallas kernels for 0%

commit v1 on v0

v1 whole, which is shorter than its diff:
```python
import functools

import jax
import jax.numpy as jnp
from jax import lax
from jax.experimental import pallas as pl
from jax.experimental.pallas import tpu as pltpu
from jax.sharding import PartitionSpec as P

HEAD = 128
BLOCK = 128
EPSILON = 1e-05
HALF_SCALE = 0.5 * HEAD ** (-0.5)
F32 = jnp.float32
BF16 = jnp.bfloat16


def head_norm(values, gain):
    centre = jnp.mean(values, axis=-1, keepdims=True)
    shifted = values - centre
    spread = jnp.mean(shifted * shifted, axis=-1, keepdims=True)
    return shifted * lax.rsqrt(spread + EPSILON) * gain


def silu_weight(scores):
    half = (scores * HALF_SCALE).astype(BF16)
    return half * jnp.tanh(half) + half


def attend(q, k, v):
    scores = lax.dot_general(q, k, (((1,), (1,)), ((), ())), preferred_element_type=F32)
    return jnp.dot(silu_weight(scores), v, preferred_element_type=F32)


def kernel(
    n_ev,
    n_hd,
    hist_len,
    cand_count,
    keys_hbm,
    values_hbm,
    queries_hbm,
    egate_hbm,
    kw_hbm,
    vw_hbm,
    egain,
    candq_hbm,
    cgate_hbm,
    cgain,
    eout,
    cout,
    keys,
    values,
    queries,
    egate,
    kw,
    vw,
    candq,
    cgate,
    own_sum,
    pair_out,
    pair_in,
    cross_out,
    cross_in,
    everyone,
    fresh_k,
    fresh_v,
    cpair_out,
    cpair_in,
    ccross_out,
    ccross_in,
    own_cand,
    load_sem,
    misc_sem,
    q_send,
    q_recv,
    pair_send,
    pair_recv,
    cross_send,
    cross_recv,
    hd_send,
    hd_recv,
    cq_send,
    cq_recv,
    cp_send,
    cp_recv,
    cc_send,
    cc_recv,
):
    n_users, hist_rows, width = keys.shape
    n_heads = width // HEAD
    rows = queries.shape[2]
    cand_rows = candq.shape[1]
    n_blocks = cand_rows // BLOCK
    n_chips = n_ev // 2
    key_tile = min(1024, hist_rows)
    ev = lax.axis_index("ev")
    hd = lax.axis_index("hd")
    chip = ev // 2
    core = ev % 2
    partner = chip * 2 + (1 - core)

    def cols(head):
        return slice(head * HEAD, (head + 1) * HEAD)

    def remote(src, dst, send, recv, **where):
        return pltpu.make_async_remote_copy(
            src_ref=src,
            dst_ref=dst,
            send_sem=send,
            recv_sem=recv,
            device_id=where,
            device_id_type=pl.DeviceIdType.MESH,
        )

    def load_keys(u):
        return pltpu.make_async_copy(keys_hbm.at[u], keys.at[u], load_sem.at[0, u])

    def load_values(u):
        return pltpu.make_async_copy(values_hbm.at[u], values.at[u], load_sem.at[1, u])

    def load_queries(u):
        return pltpu.make_async_copy(queries_hbm.at[u], queries.at[u, ev], load_sem.at[2, u])

    def load_gate(u):
        return pltpu.make_async_copy(egate_hbm.at[u], egate.at[u], load_sem.at[3, u])

    misc = [
        pltpu.make_async_copy(src, dst, misc_sem.at[i])
        for i, (src, dst) in enumerate(
            [
                (candq_hbm, candq.at[ev]),
                (kw_hbm, kw),
                (vw_hbm, vw),
                (cgate_hbm, cgate),
            ]
        )
    ]

    def q_copy(u, step, owner):
        return remote(
            queries_hbm.at[u],
            queries.at[u, owner],
            q_send.at[u, step],
            q_recv.at[u, owner],
            ev=(ev + step) % n_ev,
        )

    def cq_copy(step, owner):
        return remote(
            candq_hbm, candq.at[owner], cq_send.at[step], cq_recv.at[owner], ev=(ev + step) % n_ev
        )

    def pair_copy(u, d):
        return remote(
            pair_out.at[u, d], pair_in.at[u, d], pair_send.at[u, d], pair_recv.at[u, d], ev=partner
        )

    def cross_copy(u, d):
        return remote(
            cross_out.at[u, d],
            cross_in.at[u, d],
            cross_send.at[u, d],
            cross_recv.at[u, d],
            ev=((chip + d) % n_chips) * 2 + core,
        )

    def hd_copy(u, step, owner):
        return remote(
            everyone.at[u, owner],
            everyone.at[u, owner],
            hd_send.at[u, step],
            hd_recv.at[u, owner],
            hd=(hd + step) % n_hd,
        )

    def cpair_copy(d):
        return remote(cpair_out.at[d], cpair_in.at[d], cp_send.at[d], cp_recv.at[d], ev=partner)

    def ccross_copy(d):
        return remote(
            ccross_out.at[d],
            ccross_in.at[d],
            cc_send.at[d],
            cc_recv.at[d],
            ev=((chip + d) % n_chips) * 2 + core,
        )

    load_queries(0).start()
    load_keys(0).start()
    load_values(0).start()
    barrier = pltpu.get_barrier_semaphore()
    for step in range(1, n_ev):
        pl.semaphore_signal(
            barrier,
            inc=1,
            device_id={"ev": (ev + step) % n_ev},
            device_id_type=pl.DeviceIdType.MESH,
        )
    for step in range(1, n_hd):
        pl.semaphore_signal(
            barrier,
            inc=1,
            device_id={"hd": (hd + step) % n_hd},
            device_id_type=pl.DeviceIdType.MESH,
        )
    for u in range(1, n_users):
        load_queries(u).start()
        load_keys(u).start()
        load_values(u).start()
    for u in range(n_users):
        load_gate(u).start()
    for copy in misc:
        copy.start()
    pl.semaphore_wait(barrier, n_ev - 1 + n_hd - 1)
    for u in range(n_users):
        for step in range(1, n_ev):
            q_copy(u, step, ev).start()

    def history(u, owner):
        return [
            functools.reduce(
                lambda a, b: a + b,
                [
                    attend(
                        queries[u, owner, :, cols(head)],
                        keys[u, at : at + key_tile, cols(head)],
                        values[u, at : at + key_tile, cols(head)],
                    )
                    for at in range(0, hist_rows, key_tile)
                ],
            )
            for head in range(n_heads)
        ]

    def finish_event(u):
        load_gate(u).wait()
        for d in range(1, n_chips):
            cross_copy(u, d).wait_recv()
        for head in range(n_heads):
            total = own_sum[u, :, cols(head)]
            for d in range(1, n_chips):
                total = total + cross_in[u, d, :, cols(head)].astype(F32)
            gate = egate[u, :, cols(head)].astype(F32)
            result = (head_norm(total, egain[:, cols(head)]) * gate).astype(BF16)
            everyone[u, hd, :, cols(head)] = result
            eout[u, :, cols(head)] = result
        for step in range(1, n_hd):
            hd_copy(u, step, hd).start()

    def user_step(u, carry):
        load_keys(u).wait()
        load_values(u).wait()
        load_queries(u).wait()

        @pl.when(u == min(1, n_users - 1))
        def _():
            for step in range(1, n_ev):
                cq_copy(step, ev).start()

        live = hist_len[u] - ev * hist_rows
        for at in range(0, hist_rows, key_tile):
            spot = lax.broadcasted_iota(jnp.int32, (key_tile, HEAD), 0) + at
            mask = jnp.where(spot < live, 1.0, 0.0).astype(BF16)
            for head in range(n_heads):
                values[u, at : at + key_tile, cols(head)] = (
                    values[u, at : at + key_tile, cols(head)] * mask
                )

        def chip_step(k, carry):
            d = jnp.where(u == 0, k, n_chips - 1 - k)
            there = ((chip + d) % n_chips) * 2

            other = there + (1 - core)
            q_copy(u, 1, other).wait_recv()
            for head, part in enumerate(history(u, other)):
                pair_out[u, d, :, cols(head)] = part.astype(BF16)
            pair_copy(u, d).start()

            @pl.when(d > 0)
            def _():
                q_copy(u, 1, there + core).wait_recv()

            parts = history(u, there + core)
            pair_copy(u, d).wait_recv()
            sums = [
                part + pair_in[u, d, :, cols(head)].astype(F32)
                for head, part in enumerate(parts)
            ]

            @pl.when(d > 0)
            def _():
                for head, total in enumerate(sums):
                    cross_out[u, d, :, cols(head)] = total.astype(BF16)
                cross_copy(u, d).start()

            @pl.when(d == 0)
            def _():
                for head, total in enumerate(sums):
                    own_sum[u, :, cols(head)] = total

            @pl.when((k == 0) & (u > 0))
            def _():
                finish_event(u - 1)

            return carry

        lax.fori_loop(0, n_chips, chip_step, 0)
        return carry

    lax.fori_loop(0, n_users, user_step, 0)
    finish_event(n_users - 1)
    for copy in misc:
        copy.wait()

    def project(u, carry):
        for step in range(1, n_hd):
            hd_copy(u, 1, (hd + step) % n_hd).wait_recv()
        for weight, fresh in ((kw, fresh_k), (vw, fresh_v)):
            total = jnp.dot(everyone[u, 0], weight[0:width], preferred_element_type=F32)
            for src in range(1, n_hd):
                total = total + jnp.dot(
                    everyone[u, src],
                    weight[src * width : (src + 1) * width],
                    preferred_element_type=F32,
                )
            fresh[u] = total.astype(BF16)
        return carry

    lax.fori_loop(0, n_users, project, 0)

    counts = [cand_count[u] for u in range(n_users)]
    ends = []
    for count in counts:
        blocks = (count + (BLOCK - 1)) // BLOCK
        ends.append(blocks if not ends else ends[-1] + blocks)

    def block_owner(block):
        owner = jnp.int32(0)
        for end in ends[:-1]:
            owner = owner + jnp.where(block >= end, 1, 0)
        return owner

    def candidates(dest):
        parts = []
        for i in range(n_blocks):
            owner = block_owner(dest * n_blocks + i)
            parts.append(
                [
                    attend(
                        candq[dest, i * BLOCK : (i + 1) * BLOCK, cols(head)],
                        fresh_k[owner, :, cols(head)],
                        fresh_v[owner, :, cols(head)],
                    )
                    for head in range(n_heads)
                ]
            )
        return parts

    for step in range(1, n_ev):
        cq_copy(1, (ev + step) % n_ev).wait_recv()

    def cand_step(k, carry):
        d = n_chips - 1 - k
        there = ((chip + d) % n_chips) * 2
        for i, parts in enumerate(candidates(there + (1 - core))):
            for head, part in enumerate(parts):
                cpair_out[d, i * BLOCK : (i + 1) * BLOCK, cols(head)] = part.astype(BF16)
        cpair_copy(d).start()
        mine = candidates(there + core)
        cpair_copy(d).wait_recv()
        sums = [
            [
                part + cpair_in[d, i * BLOCK : (i + 1) * BLOCK, cols(head)].astype(F32)
                for head, part in enumerate(parts)
            ]
            for i, parts in enumerate(mine)
        ]

        @pl.when(d > 0)
        def _():
            for i, parts in enumerate(sums):
                for head, total in enumerate(parts):
                    ccross_out[d, i * BLOCK : (i + 1) * BLOCK, cols(head)] = total.astype(BF16)
            ccross_copy(d).start()

        @pl.when(d == 0)
        def _():
            for i, parts in enumerate(sums):
                for head, total in enumerate(parts):
                    own_cand[i * BLOCK : (i + 1) * BLOCK, cols(head)] = total

        return carry

    lax.fori_loop(0, n_chips, cand_step, 0)

    for d in range(1, n_chips):
        ccross_copy(d).wait_recv()
    for i in range(n_blocks):
        block = ev * n_blocks + i
        owner = block_owner(block)
        first, limit = jnp.int32(0), counts[0]
        for u in range(1, n_users):
            first = jnp.where(owner >= u, ends[u - 1], first)
            limit = jnp.where(owner >= u, counts[u], limit)
        left = limit - (block - first) * BLOCK
        spot = lax.broadcasted_iota(jnp.int32, (BLOCK, HEAD), 0)
        mask = jnp.where(spot < left, 1.0, 0.0)
        span = slice(i * BLOCK, (i + 1) * BLOCK)
        for head in range(n_heads):
            total = own_cand[span, cols(head)]
            for d in range(1, n_chips):
                total = total + ccross_in[d, span, cols(head)].astype(F32)
            gate = cgate[span, cols(head)].astype(F32)
            cout[span, cols(head)] = (head_norm(total, cgain[:, cols(head)]) * gate * mask).astype(
                BF16
            )

    def drain(u, carry):
        for step in range(1, n_ev):
            q_copy(u, step, ev).wait_send()
        for d in range(n_chips):
            pair_copy(u, d).wait_send()
        for d in range(1, n_chips):
            cross_copy(u, d).wait_send()
        for step in range(1, n_hd):
            hd_copy(u, step, hd).wait_send()
        return carry

    lax.fori_loop(0, n_users, drain, 0)
    for step in range(1, n_ev):
        cq_copy(step, ev).wait_send()
    for d in range(n_chips):
        cpair_copy(d).wait_send()
    for d in range(1, n_chips):
        ccross_copy(d).wait_send()


def local(
    n_ev,
    n_hd,
    hist_keys,
    hist_values,
    hist_len,
    new_queries,
    event_gate,
    key_weight,
    value_weight,
    event_gain,
    cand_queries,
    cand_gate,
    cand_gain,
    block_user,
    cand_count,
):
    n_users, hist_rows, width = hist_keys.shape
    rows = new_queries.shape[1]
    cand_rows = cand_queries.shape[0]
    depth = key_weight.shape[0]
    n_chips = n_ev // 2
    dma = pltpu.SemaphoreType.DMA
    vmem, anywhere, smem = (
        pl.BlockSpec(memory_space=space) for space in (pltpu.VMEM, pl.ANY, pltpu.SMEM)
    )
    scratch = [
        pltpu.VMEM((n_users, hist_rows, width), BF16),
        pltpu.VMEM((n_users, hist_rows, width), BF16),
        pltpu.VMEM((n_users, n_ev, rows, width), BF16),
        pltpu.VMEM((n_users, rows, width), BF16),
        pltpu.VMEM((depth, width), BF16),
        pltpu.VMEM((depth, width), BF16),
        pltpu.VMEM((n_ev, cand_rows, width), BF16),
        pltpu.VMEM((cand_rows, width), BF16),
        pltpu.VMEM((n_users, rows, width), F32),
        pltpu.VMEM((n_users, n_chips, rows, width), BF16),
        pltpu.VMEM((n_users, n_chips, rows, width), BF16),
        pltpu.VMEM((n_users, n_chips, rows, width), BF16),
        pltpu.VMEM((n_users, n_chips, rows, width), BF16),
        pltpu.VMEM((n_users, n_hd, rows, width), BF16),
        pltpu.VMEM((n_users, rows, width), BF16),
        pltpu.VMEM((n_users, rows, width), BF16),
        pltpu.VMEM((n_chips, cand_rows, width), BF16),
        pltpu.VMEM((n_chips, cand_rows, width), BF16),
        pltpu.VMEM((n_chips, cand_rows, width), BF16),
        pltpu.VMEM((n_chips, cand_rows, width), BF16),
        pltpu.VMEM((cand_rows, width), F32),
        dma((4, n_users)),
        dma((4,)),
        dma((n_users, n_ev)),
        dma((n_users, n_ev)),
        dma((n_users, n_chips)),
        dma((n_users, n_chips)),
        dma((n_users, n_chips)),
        dma((n_users, n_chips)),
        dma((n_users, n_hd)),
        dma((n_users, n_hd)),
        dma((n_ev,)),
        dma((n_ev,)),
        dma((n_chips,)),
        dma((n_chips,)),
        dma((n_chips,)),
        dma((n_chips,)),
    ]
    flops = 4 * n_users * rows * n_ev * hist_rows * width + 4 * n_users * rows * depth * width
    return pl.pallas_call(
        functools.partial(kernel, n_ev, n_hd),
        out_shape=(
            jax.ShapeDtypeStruct((n_users, rows, width), BF16),
            jax.ShapeDtypeStruct((cand_rows, width), BF16),
        ),
        in_specs=[smem, smem]
        + [anywhere] * 6
        + [vmem, anywhere, anywhere, vmem],
        out_specs=(vmem, vmem),
        scratch_shapes=scratch,
        cost_estimate=pl.CostEstimate(
            flops=flops,
            bytes_accessed=4 * n_users * hist_rows * width,
            transcendentals=n_users * rows * n_ev * hist_rows * (width // HEAD),
        ),
        compiler_params=pltpu.CompilerParams(
            collective_id=0, has_side_effects=True, vmem_limit_bytes=56 << 20
        ),
    )(
        hist_len,
        cand_count,
        hist_keys,
        hist_values,
        new_queries,
        event_gate,
        key_weight,
        value_weight,
        event_gain.reshape(1, width),
        cand_queries,
        cand_gate,
        cand_gain.reshape(1, width),
    )


def solution(mesh):
    return jax.shard_map(
        functools.partial(local, mesh.shape["ev"], mesh.shape["hd"]),
        mesh=mesh,
        in_specs=(
            P("grp", "ev", "hd"),
            P("grp", "ev", "hd"),
            P("grp"),
            P("grp", "ev", "hd"),
            P("grp", "ev", "hd"),
            P(None, "hd"),
            P(None, "hd"),
            P("hd"),
            P(("grp", "ev"), "hd"),
            P(("grp", "ev"), "hd"),
            P("hd"),
            P(("grp", "ev")),
            P("grp"),
        ),
        out_specs=(P("grp", "ev", "hd"), P(("grp", "ev"), "hd")),
        check_vma=False,
    )
```

time: 363 us -> 96.9 us (0.27)
  waiting for transfers between devices: 115 us -> 0 us
  local copies, waits for them, and re-layouts: 110 us -> 3.54 us
  Pallas kernels: 0 us -> 92.3 us
  matrix products: 91.5 us -> 0 us
  other arithmetic: 20.2 us -> 0 us
  between operations: 14 us -> 0.64 us
  loops' own time: 10.4 us -> 0 us
    pallas_call x0 -> x1, Pallas kernels: none -> 92.3 us  [local(): pl.pallas_call(functools.partial(kernel, n_ev, n_hd), out_shape=(jax.Shap...]
    dot_general x9 -> x0, matrix products: 91.5 us -> none  [the longest x4 78.1 us: history_step(): jnp.einsum('uhnk,ukhd->unhd', weights, values_here, preferred_element_typ...]
    all_gather x4 -> x0, waiting for transfers between devices: 68.6 us -> none  [the longest x1 46.3 us: local(): pieces = lax.all_gather(flat, 'hd', axis=1, tiled=True)]
    reduce_scatter x1 -> x0, waiting for transfers between devices: 46.3 us -> none  [local(): lax.psum_scatter(partial_sum, 'ev', scatter_dimension=1, tiled=True)]
    reshape x9 -> x0, local copies, waits for them, and re-layouts: 44.3 us -> none  [the longest x1 12.7 us: local(): hist_values.reshape(n_users, n_blocks, key_block, n_heads, HEAD)]
    dynamic_slice x12 -> x0, local copies, waits for them, and re-layouts: 43.8 us -> none  [the longest x4 25.9 us: history_step(): lax.dynamic_index_in_dim(keys_split, block_idx, 1, keepdims=False)]
    reduce_sum x4 -> x0, other arithmetic: 16 us -> none  [the longest x2 14.6 us: head_norm(): spread = jnp.mean(shifted * shifted, axis=-1, keepdims=True)]
    unnamed x31 -> x2, local copies, waits for them, and re-layouts: 14.3 us -> 3.54 us
  transfers between devices with their start and end apart: 5 -> 0, of which waited for: 5 -> 0; matrix products, arithmetic and copies ran while one was open for 14% -> 0% of each run, Pallas kernels for 0% -> 0%
where the time goes in v1:
time: 96.9 us; the launch traced here: 96.5 us
  Pallas kernels  92.3 us (95%)
  local copies, waits for them, and re-layouts  3.54 us (4%)
    pallas_call x1, Pallas kernels, local(): pl.pallas_call(functools.partial(kernel, n_ev, n_hd), out_shape=(jax.Shap...  92.3 us
    unnamed x2, local copies, waits for them, and re-layouts  3.54 us

profile of v1, /device:TPU:0, one launch (start us, length us, event | category | flops | bytes accessed | tf_op | source)
XLA Modules:
  0.0 96.5 jit_solution(6583278755674528111)
XLA Ops:
  0.6 92.3 %shard_map.131 = (bf16[4,256,256]{2,1,0:T(8,128)(2,1)}, bf16[512,256]{1,0:T(8,128)(2,1)}) custom-call(s32[4]{0:T(128)} %hist_len.1, s32[4]{0:T(128)} %cand_count.1, bf16[4,4096,256]{2,1,0:T(8,128)(2,1)} %keys_hbm.1, bf16[4,4096,256]{2,1,0:T(8,128)(2,1)} %values_hbm.1, bf16[4,256,256]{2,1,0:T(8,128)(2,1)} %queries_hbm.1, bf16[4,256,256]{2,1,0:T(8,128)(2,1)} %egate_hbm.1, ...), custom_call_target="tpu_custom_call" | custom-call | flops 18253611008 | bytes 16777216 | tf_op jit(solution)/shard_map/pallas_call | solution.py:505
  93.0 1.9 %copy.16 = bf16[4,256,256]{2,1,0:T(8,128)(2,1)} copy(bf16[4,256,256]{2,1,0:T(8,128)(2,1)} %get-tuple-element.4) | data formatting | bytes 1048576
  94.8 1.7 %copy.17 = bf16[512,256]{1,0:T(8,128)(2,1)} copy(bf16[512,256]{1,0:T(8,128)(2,1)} %get-tuple-element.5) | data formatting | bytes 524288

commit v2 on v1

--- a/solution.py
+++ b/solution.py
@@ -27,9 +27,14 @@
     return half * jnp.tanh(half) + half
 
 
-def attend(q, k, v):
+def silu_wide(scores):
+    half = scores * HALF_SCALE
+    return (half * jnp.tanh(half) + half).astype(BF16)
+
+
+def attend(q, k, v, silu=silu_weight):
     scores = lax.dot_general(q, k, (((1,), (1,)), ((), ())), preferred_element_type=F32)
-    return jnp.dot(silu_weight(scores), v, preferred_element_type=F32)
+    return jnp.dot(silu(scores), v, preferred_element_type=F32)
 
 
 def kernel(
@@ -82,6 +87,8 @@
     hd_recv,
     cq_send,
     cq_recv,
+    qf_send,
+    cqf_send,
     cp_send,
     cp_recv,
     cc_send,
@@ -137,19 +144,45 @@
         )
     ]
 
-    def q_copy(u, step, owner):
+    def device(d, flip):
+        return ((chip + d) % n_chips) * 2 + (1 - core if flip else core)
+
+    def q_copy(u, d, flip, owner):
         return remote(
             queries_hbm.at[u],
             queries.at[u, owner],
-            q_send.at[u, step],
+            q_send.at[u, 2 * d + flip],
             q_recv.at[u, owner],
-            ev=(ev + step) % n_ev,
-        )
-
-    def cq_copy(step, owner):
-        return remote(
-            candq_hbm, candq.at[owner], cq_send.at[step], cq_recv.at[owner], ev=(ev + step) % n_ev
-        )
+            ev=device(d, flip),
+        )
+
+    def q_forward(u, d):
+        owner = device(d, 0)
+        return remote(
+            queries.at[u, owner],
+            queries.at[u, owner],
+            qf_send.at[u, d],
+            q_recv.at[u, owner],
+            ev=partner,
+        )
+
+    def cq_copy(d, flip, owner):
+        return remote(
+            candq_hbm,
+            candq.at[owner],
+            cq_send.at[2 * d + flip],
+            cq_recv.at[owner],
+            ev=device(d, flip),
+        )
+
+    def cq_forward(d):
+        owner = device(d, 0)
+        return remote(
+            candq.at[owner], candq.at[owner], cqf_send.at[d], cq_recv.at[owner], ev=partner
+        )
+
+    others = [(0, 1)] + [(d, flip) for d in range(1, n_chips) for flip in (0, 1)]
+    firsts = [(0, 1)] + [(d, 0) for d in range(1, n_chips)]
 
     def pair_copy(u, d):
         return remote(
@@ -165,14 +198,34 @@
             ev=((chip + d) % n_chips) * 2 + core,
         )
 
-    def hd_copy(u, step, owner):
+    def hd_copy(u, left, owner):
         return remote(
             everyone.at[u, owner],
             everyone.at[u, owner],
-            hd_send.at[u, step],
+            hd_send.at[u, left, owner],
             hd_recv.at[u, owner],
-            hd=(hd + step) % n_hd,
-        )
+            hd=hd - 1 if left else hd + 1,
+        )
+
+    def hd_pass(u, far, act):
+        @pl.when((hd >= far) & (hd < n_hd - 1))
+        def _():
+            act(hd_copy(u, 0, hd - far))
+
+        @pl.when((hd + far <= n_hd - 1) & (hd > 0))
+        def _():
+            act(hd_copy(u, 1, hd + far))
+
+    def hd_hop(u, far):
+        @pl.when(hd >= far)
+        def _():
+            hd_copy(u, 0, hd - far).wait_recv()
+
+        @pl.when(hd + far <= n_hd - 1)
+        def _():
+            hd_copy(u, 0, hd + far).wait_recv()
+
+        hd_pass(u, far, lambda copy: copy.start())
 
     def cpair_copy(d):
         return remote(cpair_out.at[d], cpair_in.at[d], cp_send.at[d], cp_recv.at[d], ev=partner)
@@ -214,8 +267,8 @@
         copy.start()
     pl.semaphore_wait(barrier, n_ev - 1 + n_hd - 1)
     for u in range(n_users):
-        for step in range(1, n_ev):
-            q_copy(u, step, ev).start()
+        for d, flip in firsts if u else others:
+            q_copy(u, d, flip, ev).start()
 
     def history(u, owner):
         return [
@@ -245,8 +298,7 @@
             result = (head_norm(total, egain[:, cols(head)]) * gate).astype(BF16)
             everyone[u, hd, :, cols(head)] = result
             eout[u, :, cols(head)] = result
-        for step in range(1, n_hd):
-            hd_copy(u, step, hd).start()
+        hd_pass(u, 0, lambda copy: copy.start())
 
     def user_step(u, carry):
         load_keys(u).wait()
@@ -255,8 +307,8 @@
 
         @pl.when(u == min(1, n_users - 1))
         def _():
-            for step in range(1, n_ev):
-                cq_copy(step, ev).start()
+            for d, flip in firsts:
+                cq_copy(d, flip, ev).start()
 
         live = hist_len[u] - ev * hist_rows
         for at in range(0, hist_rows, key_tile):
@@ -272,14 +324,30 @@
             there = ((chip + d) % n_chips) * 2
 
             other = there + (1 - core)
-            q_copy(u, 1, other).wait_recv()
+            q_copy(u, 0, 1, other).wait_recv()
             for head, part in enumerate(history(u, other)):
                 pair_out[u, d, :, cols(head)] = part.astype(BF16)
             pair_copy(u, d).start()
 
-            @pl.when(d > 0)
-            def _():
-                q_copy(u, 1, there + core).wait_recv()
+            @pl.when((d > 0) & (u == 0))
+            def _():
+                q_copy(u, 0, 1, there + core).wait_recv()
+
+            @pl.when((k == n_chips - 1) & (u < n_users - 1))
+            def _():
+                for far in range(1, n_chips):
+                    q_copy(u + 1, 0, 1, device(far, 0)).wait_recv()
+                    q_forward(u + 1, far).start()
+
+            @pl.when((k == n_chips - 1) & (u == n_users - 1))
+            def _():
+                for far in range(1, n_chips):
+                    cq_copy(0, 1, device(far, 0)).wait_recv()
+                    cq_forward(far).start()
+
+            @pl.when((k == n_chips - 1) & (u > 0))
+            def _():
+                hd_hop(u - 1, 1)
 
             parts = history(u, there + core)
             pair_copy(u, d).wait_recv()
@@ -303,6 +371,11 @@
             def _():
                 finish_event(u - 1)
 
+            @pl.when((k == n_chips - 1) & (u > 0))
+            def _():
+                for far in range(2, n_hd - 1):
+                    hd_hop(u - 1, far)
+
             return carry
 
         lax.fori_loop(0, n_chips, chip_step, 0)
@@ -313,9 +386,7 @@
     for copy in misc:
         copy.wait()
 
-    def project(u, carry):
-        for step in range(1, n_hd):
-            hd_copy(u, 1, (hd + step) % n_hd).wait_recv()
+    def project(u):
         for weight, fresh in ((kw, fresh_k), (vw, fresh_v)):
             total = jnp.dot(everyone[u, 0], weight[0:width], preferred_element_type=F32)
             for src in range(1, n_hd):
@@ -325,9 +396,15 @@
                     preferred_element_type=F32,
                 )
             fresh[u] = total.astype(BF16)
-        return carry
-
-    lax.fori_loop(0, n_users, project, 0)
+
+    for u in range(max(n_users - 1, n_hd - 1)):
+        if u < n_users - 1:
+            if n_hd > 2:
+                hd_hop(u, n_hd - 1)
+            project(u)
+        if u < n_hd - 1:
+            hd_hop(n_users - 1, u + 1)
+    project(n_users - 1)
 
     counts = [cand_count[u] for u in range(n_users)]
     ends = []
@@ -351,14 +428,15 @@
                         candq[dest, i * BLOCK : (i + 1) * BLOCK, cols(head)],
                         fresh_k[owner, :, cols(head)],
                         fresh_v[owner, :, cols(head)],
+                        silu_wide,
                     )
                     for head in range(n_heads)
                 ]
             )
         return parts
 
-    for step in range(1, n_ev):
-        cq_copy(1, (ev + step) % n_ev).wait_recv()
+    for d in range(n_chips):
+        cq_copy(0, 1, device(d, 1)).wait_recv()
 
     def cand_step(k, carry):
         d = n_chips - 1 - k
@@ -416,20 +494,21 @@
                 BF16
             )
 
-    def drain(u, carry):
-        for step in range(1, n_ev):
-            q_copy(u, step, ev).wait_send()
+    for u in range(n_users):
+        for d, flip in firsts if u else others:
+            q_copy(u, d, flip, ev).wait_send()
+        for d in range(1, n_chips):
+            if u:
+                q_forward(u, d).wait_send()
+            cross_copy(u, d).wait_send()
         for d in range(n_chips):
             pair_copy(u, d).wait_send()
-        for d in range(1, n_chips):
-            cross_copy(u, d).wait_send()
-        for step in range(1, n_hd):
-            hd_copy(u, step, hd).wait_send()
-        return carry
-
-    lax.fori_loop(0, n_users, drain, 0)
-    for step in range(1, n_ev):
-        cq_copy(step, ev).wait_send()
+        for far in range(n_hd - 1):
+            hd_pass(u, far, lambda copy: copy.wait_send())
+    for d, flip in firsts:
+        cq_copy(d, flip, ev).wait_send()
+    for d in range(1, n_chips):
+        cq_forward(d).wait_send()
     for d in range(n_chips):
         cpair_copy(d).wait_send()
     for d in range(1, n_chips):
@@ -492,10 +571,12 @@
         dma((n_users, n_chips)),
         dma((n_users, n_chips)),
         dma((n_users, n_chips)),
-        dma((n_users, n_hd)),
+        dma((n_users, 2, n_hd)),
         dma((n_users, n_hd)),
         dma((n_ev,)),
         dma((n_ev,)),
+        dma((n_users, n_chips)),
+        dma((n_chips,)),
         dma((n_chips,)),
         dma((n_chips,)),
         dma((n_chips,)),

time: 96.9 us -> 91.5 us (0.944)
  Pallas kernels: 92.3 us -> 87.1 us
    pallas_call x1, Pallas kernels: 92.3 us -> 87.1 us  [local(): pl.pallas_call(functools.partial(kernel, n_ev, n_hd), out_shape=(jax.Shap...]
where the time goes in v2:
time: 91.5 us; the launch traced here: 91.2 us
  Pallas kernels  87.1 us (95%)
  local copies, waits for them, and re-layouts  3.54 us (4%)
    pallas_call x1, Pallas kernels, local(): pl.pallas_call(functools.partial(kernel, n_ev, n_hd), out_shape=(jax.Shap...  87.1 us
    unnamed x2, local copies, waits for them, and re-layouts  3.54 us

profile of v2, /device:TPU:0, one launch (start us, length us, event | category | flops | bytes accessed | tf_op | source)
XLA Modules:
  0.0 91.2 jit_solution(15955667440252121252)
XLA Ops:
  0.6 87.1 %shard_map.131 = (bf16[4,256,256]{2,1,0:T(8,128)(2,1)}, bf16[512,256]{1,0:T(8,128)(2,1)}) custom-call(s32[4]{0:T(128)} %hist_len.1, s32[4]{0:T(128)} %cand_count.1, bf16[4,4096,256]{2,1,0:T(8,128)(2,1)} %keys_hbm.1, bf16[4,4096,256]{2,1,0:T(8,128)(2,1)} %values_hbm.1, bf16[4,256,256]{2,1,0:T(8,128)(2,1)} %queries_hbm.1, bf16[4,256,256]{2,1,0:T(8,128)(2,1)} %egate_hbm.1, ...), custom_call_target="tpu_custom_call" | custom-call | flops 18253611008 | bytes 16777216 | tf_op jit(solution)/shard_map/pallas_call | solution.py:586
  87.7 1.9 %copy.16 = bf16[4,256,256]{2,1,0:T(8,128)(2,1)} copy(bf16[4,256,256]{2,1,0:T(8,128)(2,1)} %get-tuple-element.4) | data formatting | bytes 1048576
  89.6 1.7 %copy.17 = bf16[512,256]{1,0:T(8,128)(2,1)} copy(bf16[512,256]{1,0:T(8,128)(2,1)} %get-tuple-element.5) | data formatting | bytes 524288
